TPU v7x, 128 devices: a whole 4x4x4 slice. The times are simulated.
128 devices in a mesh: sub: 32 (over z, x, core), col: 4 (over y).
Axes of the slice: x: 4, y: 4, z: 4, core: 2. Of those that a mesh axis runs over, the one named last changes fastest.
Arguments:
- elem_records: bfloat16 [32768, 1152], P(('sub', 'col')), may hold values from -0.119628906 to 0.119628906
- elem_owner: int32 [32768, 1], P(('sub', 'col')), may hold values from 0 to 31; in each aligned block of 256 rows (0 to 255, 256 to 511, ...) at most 16 rows name the same one
- elem_block: int32 [32768], P(('sub', 'col')), may hold values from 0 to 255
- elem_offset: int32 [32768], P(('sub', 'col')), may hold values from 0 to 5
- modes: bfloat16 [512, 64, 512], P('sub', None, 'col'), may hold values from -0.59765625 to 0.59765625
- mode_readers: int32 [512, 2], P('sub'), may hold values from 0 to 31, all different within a row; in each aligned block of 16 rows (0 to 15, 16 to 31, ...) at most 2 rows name the same one
- pattern: int32 [2048, 4], P('sub'), may hold values from 0 to 63
Outputs:
- gram_stiff: float32 [512, 512], P('sub', 'col')
- gram_mass: float32 [512, 512], P('sub', 'col')
Inputs may be any that keep to these rules, and one draw needn't show every extreme that they name: `elem_owner`: the rows of one device name one subdomain at most 16 times, and in every draw some subdomain exactly 16 times. `mode_readers`: each row names two different subdomains; the rows of one index of sub name one subdomain at most 2 times, and in every draw some subdomain exactly 2 times.
All inputs are finite; a program needn't handle non-finite values.
Results may differ from a plain program's by a relative error of at most 0.0038.
Values may be sent and summed in bfloat16 or wider, within the bound.
A program may use at most 192 MiB of HBM per device.

v0:
```python
import jax
import jax.numpy as jnp
from jax import lax
from jax.sharding import PartitionSpec as P

MODES = 512
BS = 64
EDOF = 24
NNZ = 4
E_DEV = 256
NQ = 64
KW = 1152


def send_positions(targets, peer_count, capacity):
    matches = (targets[:, None] == jnp.arange(peer_count, dtype=jnp.int32)[None, :]).astype(
        jnp.int32
    )
    ranks = jnp.sum((jnp.cumsum(matches, axis=0) - 1) * matches, axis=1)
    return targets * capacity + ranks


def assemble(all_records, all_places):
    block_total = NQ * NNZ
    row_ids = all_places[:, 0] * 6 + all_places[:, 1]
    summed = (
        jnp.zeros((block_total * 6, KW), jnp.float32)
        .at[row_ids]
        .add(all_records.astype(jnp.float32))
    )
    summed = summed.reshape(block_total, 6, 2, EDOF, EDOF)
    result = jnp.zeros((2, block_total, BS, BS), jnp.float32)
    for offset_step in range(6):
        piece = jnp.transpose(summed[:, offset_step], (1, 0, 2, 3))
        low = 8 * offset_step
        result = result.at[:, :, low : low + EDOF, low : low + EDOF].add(piece)
    return result.reshape(2, NQ, NNZ, BS, BS).astype(jnp.bfloat16)


def body(elem_records, elem_owner, elem_block, elem_offset, modes, mode_readers, pattern):
    sub_count = lax.axis_size("sub")
    elem_slots = 2 * E_DEV // sub_count
    mode_slots = NQ // sub_count
    local_cols = modes.shape[2]
    positions = send_positions(elem_owner[:, 0], sub_count, elem_slots)
    send_records = (
        jnp.zeros((sub_count * elem_slots, KW), jnp.bfloat16).at[positions].set(elem_records)
    )
    places = jnp.stack([elem_block, elem_offset], axis=1)
    send_places = jnp.zeros((sub_count * elem_slots, 2), jnp.int32).at[positions].set(places)
    got_records, got_places = (
        lax.all_to_all(
            send_records.reshape(sub_count, elem_slots, KW),
            "sub",
            split_axis=0,
            concat_axis=0,
            tiled=True,
        ),
        lax.all_to_all(
            send_places.reshape(sub_count, elem_slots, 2),
            "sub",
            split_axis=0,
            concat_axis=0,
            tiled=True,
        ),
    )
    all_records, all_places = (
        lax.all_gather(got_records, "col", axis=0, tiled=True),
        lax.all_gather(got_places, "col", axis=0, tiled=True),
    )
    all_records = all_records.reshape(-1, KW)
    all_places = all_places.reshape(-1, 2)
    readers_flat = mode_readers.reshape(-1)
    mode_positions = send_positions(readers_flat, sub_count, mode_slots)
    source_blocks = jnp.arange(readers_flat.shape[0], dtype=jnp.int32) // 2
    send_modes = (
        jnp.zeros((sub_count * mode_slots, BS, local_cols), jnp.bfloat16)
        .at[mode_positions]
        .set(modes[source_blocks])
    )
    stiff_mass = assemble(all_records, all_places)
    slot_modes = lax.all_to_all(
        send_modes.reshape(sub_count, mode_slots, BS, local_cols),
        "sub",
        split_axis=0,
        concat_axis=0,
        tiled=True,
    ).reshape(NQ, BS, local_cols)
    gathered = slot_modes[pattern]
    products = jnp.einsum(
        "crjab,rjbm->cram", stiff_mass, gathered, preferred_element_type=jnp.float32
    ).astype(jnp.bfloat16)
    product_rows = products.reshape(2, NQ * BS, local_cols)
    mode_rows = slot_modes.reshape(NQ * BS, local_cols)
    gram_term = jnp.einsum(
        "ra,crm->acm",
        lax.all_gather(mode_rows, "col", axis=1, tiled=True),
        product_rows,
        preferred_element_type=jnp.float32,
    )
    share_rows = MODES // sub_count
    gram_total = lax.psum(gram_term, "sub")
    mine = lax.dynamic_slice_in_dim(gram_total, lax.axis_index("sub") * share_rows, share_rows, 0)
    return (mine[:, 0, :], mine[:, 1, :])


def solution(mesh):
    in_specs = (
        P(("sub", "col"), None),
        P(("sub", "col"), None),
        P(("sub", "col")),
        P(("sub", "col")),
        P("sub", None, "col"),
        P("sub", None),
        P("sub", None),
    )
    out_specs = (P("sub", "col"), P("sub", "col"))
    return jax.shard_map(body, mesh=mesh, in_specs=in_specs, out_specs=out_specs, check_vma=False)
```

profile of v0, /device:TPU:1, one launch (start us, length us, event | category | flops | bytes accessed | tf_op | source)
XLA Modules:
  0.0 363.1 jit_solution(15174351066579213494)
XLA Ops:
  10.2 2.6 scatter_custom_fusion.2
  12.8 28.2 %all_to_all.15 = bf16[32,16,1152]{2,1,0:T(8,128)(2,1)} all-to-all(bf16[32,16,1152]{2,1,0:T(8,128)(2,1)S(1)} %bitcast.92), channel_id=1, replica_groups=mesh['sub'=32,'col'=4] {'sub'}, dimensions={0} | all-to-all | bytes 2359296 | tf_op jit(solution)/shard_map/all_to_all | solution.py:52
  44.3 20.8 %all_to_all.16 = bf16[32,2,64,128]{3,2,1,0:T(8,128)(2,1)S(1)} all-to-all(bf16[32,2,64,128]{3,2,1,0:T(8,128)(2,1)S(1)} %bitcast.90), channel_id=1, replica_groups=mesh['sub'=32,'col'=4] {'sub'}, dimensions={0} | all-to-all | bytes 2097152 | tf_op jit(solution)/shard_map/all_to_all | solution.py:82
  68.8 3.9 %all-to-all-start.1 = ((s32[32,16,2]{1,2,0:T(2,128)}), s32[32,16,2]{1,2,0:T(2,128)S(1)}, u32[]{:S(2)}, u32[]{:S(2)}) async-start(s32[32,16,2]{1,2,0:T(2,128)} %copy.85), calls=%async_computation.1 | async-start | bytes 65536 | tf_op jit(solution)/shard_map/all_to_all | solution.py:59
  72.9 7.1 %all-to-all-done.1 = s32[32,16,2]{1,2,0:T(2,128)S(1)} async-done(((s32[32,16,2]{1,2,0:T(2,128)}), s32[32,16,2]{1,2,0:T(2,128)S(1)}, u32[]{:S(2)}, u32[]{:S(2)}) %all-to-all-start.1) | async-done | bytes 4128 | tf_op jit(solution)/shard_map/all_to_all | solution.py:59
  80.0 11.3 %all_gather.10 = s32[128,16,2]{1,2,0:T(2,128)S(1)} all-gather(s32[32,16,2]{1,2,0:T(2,128)S(1)} %all-to-all-done.1), channel_id=1, replica_groups=mesh['sub'=32,'col'=4] {'col'}, dimensions={0}, use_global_device_ids=true | all-gather | bytes 20480 | tf_op jit(solution)/shard_map/all_gather | solution.py:69
  91.4 3.1 gather_fusion.1
  94.5 23.6 %scatter_custom_fusion.3 = f32[1536,1152]{1,0:T(8,128)} fusion(s32[2048]{0:T(1024)S(1)} %bitcast.98, bf16[2048,1152]{1,0:T(8,128)(2,1)} %bitcast.91, f32[]{:T(128)} %constant.229.clone.1), kind=kCustom, calls=%fused_computation.6 | custom fusion | flops 4718592 | bytes 11796484 | tf_op jit(solution)/shard_map/scatter-add | solution.py:29
  118.1 27.3 %reshape.359 = f32[256,6,2,24,24]{4,3,2,1,0:T(8,128)} reshape(f32[1536,1152]{1,0:T(8,128)} %scatter_custom_fusion.3) | data formatting | bytes 14155776 | tf_op jit(solution)/shard_map/reshape | solution.py:31
  145.4 25.8 %fusion.28 = (f32[256,1,2,24,24]{4,3,2,1,0:T(8,128)}, f32[256,1,2,24,24]{4,3,2,1,0:T(8,128)}, f32[256,1,2,24,24]{4,3,2,1,0:T(8,128)}, f32[256,1,2,24,24]{4,3,2,1...) fusion(f32[256,6,2,24,24]{4,3,2,1,0:T(8,128)} %reshape.359), kind=kLoop, calls=%fused_computation.61 | loop fusion | bytes 14155776 | tf_op jit(solution)/shard_map/slice | solution.py:34
  171.2 5.1 %copy.100 = f32[256,1,2,24,24]{0,4,3,2,1:T(8,128)S(1)} copy(f32[256,1,2,24,24]{4,3,2,1,0:T(8,128)} %get-tuple-element.79) | data formatting | bytes 2359296
  176.3 4.3 %scatter-add.29 = f32[2,256,64,64]{1,3,2,0:T(8,128)} pad(f32[2,256,24,24]{1,3,2,0:T(8,128)S(1)} %bitcast.87, f32[]{:T(128)} %constant.229.clone.1), padding=0_0x0_0x0_40x0_40 | pad | bytes 9568260 | tf_op jit(solution)/shard_map/scatter-add | solution.py:36
  180.6 6.0 %copy.101 = f32[256,1,2,24,24]{0,4,3,2,1:T(8,128)} copy(f32[256,1,2,24,24]{4,3,2,1,0:T(8,128)} %get-tuple-element.78) | data formatting | bytes 2359296
  186.6 6.0 %copy.102 = f32[256,1,2,24,24]{0,4,3,2,1:T(8,128)} copy(f32[256,1,2,24,24]{4,3,2,1,0:T(8,128)} %get-tuple-element.77) | data formatting | bytes 2359296
  192.6 6.0 %copy.103 = f32[256,1,2,24,24]{0,4,3,2,1:T(8,128)} copy(f32[256,1,2,24,24]{4,3,2,1,0:T(8,128)} %get-tuple-element.76) | data formatting | bytes 2359296
  198.5 5.1 %copy.104 = f32[256,1,2,24,24]{0,4,3,2,1:T(8,128)S(1)} copy(f32[256,1,2,24,24]{4,3,2,1,0:T(8,128)} %get-tuple-element.75) | data formatting | bytes 2359296
  203.6 6.0 %copy.105 = f32[256,1,2,24,24]{0,4,3,2,1:T(8,128)} copy(f32[256,1,2,24,24]{4,3,2,1,0:T(8,128)} %get-tuple-element.74) | data formatting | bytes 2359296
  212.1 2.9 fusion.17
  215.0 2.5 fusion.16
  222.5 6.0 %convert_element_type.30 = bf16[2,256,64,64]{1,3,2,0:T(8,128)(2,1)} convert(f32[2,256,64,64]{1,3,2,0:T(8,128)} %fusion.14) | non-fusion elementwise | flops 2097152 | bytes 12582912 | tf_op jit(solution)/shard_map/convert_element_type | solution.py:37
  228.5 13.0 %copy.93 = bf16[2,256,64,64]{3,2,1,0:T(8,128)(2,1)} copy(bf16[2,256,64,64]{1,3,2,0:T(8,128)(2,1)} %convert_element_type.30) | data formatting | bytes 8388608 | tf_op jit(solution)/shard_map/convert_element_type | solution.py:37
  241.5 6.8 %fusion.9 = bf16[2,64,64,128]{3,2,0,1:T(8,128)(2,1)S(1)} fusion(bf16[64,4,64,128,1]{3,2,1,4,0:T(8,128)(2,1)} %bitcast.93, bf16[2,64,4,64,64]{4,3,2,1,0:T(8,128)(2,1)} %bitcast.89), kind=kOutput, calls=%fused_computation.15 | convolution fusion | flops 537919488 | bytes 10485760 | tf_op jit(solution)/shard_map/crjab,rjbm->cram/dot_general | solution.py:90
  248.5 4.2 %fusion.4 = f32[512,2,128]{2,0,1:T(8,128)} fusion(bf16[2,4096,128]{2,1,0:T(8,128)(2,1)S(1)} %bitcast.94, bf16[4096,512]{0,1:T(8,128)(2,1)} %all-gather.3.cloned.1.call-done), kind=kOutput, calls=%fused_computation.11 | convolution fusion | flops 1073741824 | bytes 6815744 | tf_op jit(solution)/shard_map/ra,crm->acm/dot_general | solution.py:95
  252.8 102.4 %all-reduce.3.cloned.1.call-done = f32[512,2,128]{2,0,1:T(8,128)} async-done(((f32[512,2,128]{2,0,1:T(8,128)}), f32[512,2,128]{2,0,1:T(8,128)}) %all-reduce.3.cloned.1.call-update) | async-done | bytes 524304 | tf_op jit(solution)/shard_map/psum | solution.py:102
  (61 shorter events, 19.2 us)
Async XLA Ops:
  7.2 34.7 %copy-start = (bf16[16,64,128]{2,1,0:T(8,128)(2,1)S(1)}, bf16[16,64,128]{2,1,0:T(8,128)(2,1)}, u32[]{:S(2)}) copy-start(bf16[16,64,128]{2,1,0:T(8,128)(2,1)} %param.23) | copy-start | bytes 786436
  7.2 33.9 %copy-start.4 = (s32[16,2]{0,1:T(2,128)S(1)}, s32[16,2]{0,1:T(2,128)}, u32[]{:S(2)}) copy-start(s32[16,2]{0,1:T(2,128)} %param.24) | copy-start | bytes 388
  7.2 87.3 %all-gather.5.cloned.1.call-start = ((), (), s32[]{:S(2)}) async-start(), calls=%async_computation.4 | async-start | bytes 5898240 | tf_op jit(solution)/shard_map/all_gather | solution.py:68
  41.0 25.5 %copy-start.6 = (s32[256]{0:T(256)S(1)}, s32[256]{0:T(256)}, u32[]{:S(2)}) copy-start(s32[256]{0:T(256)} %param.22) | copy-start | bytes 3076
  41.0 25.5 %copy-start.7 = (s32[256]{0:T(256)S(1)}, s32[256]{0:T(256)}, u32[]{:S(2)}) copy-start(s32[256]{0:T(256)} %param.21) | copy-start | bytes 3076
  41.1 207.5 %all-gather.3.cloned.1.call-start = ((), (), s32[]{:S(2)}) async-start(), calls=%async_computation.3 | async-start | bytes 5242880 | tf_op jit(solution)/shard_map/all_gather | solution.py:97
  41.8 30.9 %copy-start.5 = (s32[64,4]{0,1:T(4,128)S(1)}, s32[64,4]{0,1:T(4,128)}, u32[]{:S(2)}) copy-start(s32[64,4]{0,1:T(4,128)} %param.25) | copy-start | bytes 3076
  68.8 11.3 %all-to-all-start.1 = ((s32[32,16,2]{1,2,0:T(2,128)}), s32[32,16,2]{1,2,0:T(2,128)S(1)}, u32[]{:S(2)}, u32[]{:S(2)}) async-start(s32[32,16,2]{1,2,0:T(2,128)} %copy.85), calls=%async_computation.1 | async-start | bytes 65536 | tf_op jit(solution)/shard_map/all_to_all | solution.py:59
  72.7 282.6 %all-reduce.3.cloned.1.call-start = ((), (), s32[]{:S(2)}) async-start(), calls=%async_computation.5 | async-start | bytes 1048576 | tf_op jit(solution)/shard_map/psum | solution.py:102
  209.6 5.4 %copy-start.3 = (f32[256,1,2,24,24]{0,4,3,2,1:T(8,128)S(1)}, f32[256,1,2,24,24]{0,4,3,2,1:T(8,128)}, u32[]{:S(2)}) copy-start(f32[256,1,2,24,24]{0,4,3,2,1:T(8,128)} %copy.103) | copy-start | bytes 3538948
  212.1 7.9 %copy-start.2 = (f32[256,1,2,24,24]{0,4,3,2,1:T(8,128)S(1)}, f32[256,1,2,24,24]{0,4,3,2,1:T(8,128)}, u32[]{:S(2)}) copy-start(f32[256,1,2,24,24]{0,4,3,2,1:T(8,128)} %copy.105) | copy-start | bytes 3538948
  248.3 108.2 %copy-start.1 = (bf16[16,64,128]{2,1,0:T(8,128)(2,1)S(1)}, bf16[16,64,128]{2,1,0:T(8,128)(2,1)}, u32[]{:S(2)}) copy-start(bf16[16,64,128]{2,1,0:T(8,128)(2,1)} %param.23) | copy-start | bytes 786436
Sparse Core Ops, SparseCore 0:
  41.1 51.1 all-gather.4
  94.0 48.8 all-gather.2
  252.9 102.2 all-reduce.2
where the time goes:
time: 365 us; the launch traced here: 363 us
  local copies, waits for them, and re-layouts  119 us (33%)
  waiting for transfers between devices  110 us (30%)
  blocking collectives  60.3 us (17%)
  other arithmetic  45.7 us (13%)
  between operations  14 us (4%)
  matrix products  11 us (3%)
  starting transfers between devices  4.01 us (1%)
    psum x1, waiting for transfers between devices, body(): gram_total = lax.psum(gram_term, 'sub')  102 us
    unnamed x23, local copies, waits for them, and re-layouts  34.2 us
    all_to_all x1, blocking collectives, body(): lax.all_to_all(send_records.reshape(sub_count, elem_slots, KW), 'sub', sp...  28.2 us
    reshape x1, local copies, waits for them, and re-layouts, assemble(): summed = summed.reshape(block_total, 6, 2, EDOF, EDOF)  27.3 us
    slice x1, local copies, waits for them, and re-layouts, assemble(): piece = jnp.transpose(summed[:, offset_step], (1, 0, 2, 3))  25.8 us
    scatter-add x1, other arithmetic, assemble(): summed = jnp.zeros((block_total * 6, KW), jnp.float32).at[row_ids].add(al...  23.6 us
    all_to_all x1, blocking collectives, body(): lax.all_to_all(send_modes.reshape(sub_count, mode_slots, BS, local_cols),...  20.8 us
    convert_element_type x1, local copies, waits for them, and re-layouts, assemble(): return result.reshape(2, NQ, NNZ, BS, BS).astype(jnp.bfloat16)  13 us
  transfers between devices with their start and end apart: 4, of which 2 were waited for; matrix products, arithmetic and copies ran while one was open for 45% of the time, Pallas kernels for 0%

commit v1 on v0

v1 whole, which is shorter than its diff:
```python
import functools

import jax
import jax.numpy as jnp
from jax import lax
from jax.experimental import pallas as pl
from jax.experimental.pallas import tpu as pltpu
from jax.sharding import PartitionSpec as P

MESH = pl.DeviceIdType.MESH
BF16 = jnp.bfloat16
F32 = jnp.float32
I32 = jnp.int32

BS = 64
NQ = 64
NNZ = 4
KW = 1152
KA = 1280
COLS = 128
SLOTS_E = 16


def dot(a, b):
    return jnp.dot(a, b, preferred_element_type=F32)


def dot_nt(a, b):
    return lax.dot_general(a, b, (((1,), (1,)), ((), ())), preferred_element_type=F32)


def kernel(
    midx, pat, rec, place, owner_row, owner_col, modes,
    stiff, mass,
    send_m, x0, xl, xr, xo, send_r, rbuf, ebuf, mbuf, ks, lb, xt, pb, gst, d0, hs, hr, tot, tr,
    sm_send, sm_recv, sr_send, sr_recv, fr_send, fl_send, xl_recv, xr_recv,
    rr_send, rl_send, xoa_recv, xob_recv, d_send, d_recv, h_send, h_recv, t_send, t_recv,
):
    me = lax.axis_index("sub")
    y = lax.axis_index("col")
    core = lax.rem(me, 2)
    p = me // 2
    z = p // 4
    x = lax.rem(p, 4)
    sib = p * 2 + 1 - core
    right = lax.rem(y + 1, 4)
    left = lax.rem(y + 3, 4)
    opp = lax.rem(y + 2, 4)

    def chip_at(g):
        return lax.rem(z + g // 4, 4) * 4 + lax.rem(x + lax.rem(g, 4), 4)

    def chip_from(g):
        return lax.rem(z + 4 - g // 4, 4) * 4 + lax.rem(x + 4 - lax.rem(g, 4), 4)

    def remote(src, dst, ssem, rsem, dev):
        return pltpu.make_async_remote_copy(
            src_ref=src, dst_ref=dst, send_sem=ssem, recv_sem=rsem, device_id=dev, device_id_type=MESH
        )

    def wait_bytes(ref, sem):
        pltpu.make_async_copy(ref, ref, sem).wait()

    barrier = pltpu.get_barrier_semaphore()
    pl.semaphore_signal(barrier, inc=1, device_id=(sib, y), device_id_type=MESH)
    for yy in (left, right, opp):
        pl.semaphore_signal(barrier, inc=1, device_id=(me, yy), device_id_type=MESH)

    def greet(g, _):
        q = chip_at(g)
        for cc in range(2):
            pl.semaphore_signal(barrier, inc=1, device_id=(q * 2 + cc, y), device_id_type=MESH)
        return 0

    lax.fori_loop(1, 16, greet, 0)

    def fill(s, _):
        k = midx[s]
        block = modes[jnp.maximum(k, 0)]
        send_m[s] = jnp.where(k >= 0, block, jnp.zeros_like(block))
        return 0

    lax.fori_loop(0, NQ, fill, 0, unroll=4)
    pl.semaphore_wait(barrier, 34)

    x0[pl.ds(2 * me, 2)] = send_m[pl.ds(2 * me, 2)]

    def send_mode(dest):
        remote(
            send_m.at[pl.ds(2 * dest, 2)], x0.at[pl.ds(2 * me, 2)], sm_send, sm_recv.at[p], (dest, y)
        ).start()

    send_mode(sib)

    def send_modes(g, _):
        q = chip_at(g)
        for cc in range(2):
            send_mode(q * 2 + cc)
        return 0

    lax.fori_loop(1, 16, send_modes, 0)

    before = lax.broadcasted_iota(I32, (256, 256), 0) < lax.broadcasted_iota(I32, (256, 256), 1)
    same = owner_col[...] == owner_row[...]
    rank = jnp.sum(jnp.where(same & before, 1, 0), axis=0, keepdims=True)
    pos = owner_row[...] * SLOTS_E + rank

    def permute(g, _):
        rows = lax.broadcasted_iota(I32, (128, 256), 0) + g * 128
        pick = jnp.where(rows == pos, 1.0, 0.0).astype(BF16)
        at = pl.ds(pl.multiple_of(g * 128, 128), 128)
        send_r[at, 0:KW] = dot(pick, rec[...]).astype(BF16)
        send_r[at, KW:KA] = dot(pick, place[...]).astype(BF16)
        return 0

    lax.fori_loop(0, 4, permute, 0)

    def rows16(d):
        return pl.ds(pl.multiple_of(d * 16, 16), 16)

    rbuf[rows16(me)] = send_r[rows16(me)]

    def send_rec(dest):
        remote(send_r.at[rows16(dest)], rbuf.at[rows16(me)], sr_send, sr_recv, (dest, y)).start()

    send_rec(sib)

    def send_recs(g, _):
        q = chip_at(g)
        for cc in range(2):
            send_rec(q * 2 + cc)
        return 0

    lax.fori_loop(1, 16, send_recs, 0)

    def forward(q):
        at = pl.ds(4 * q, 4)
        remote(x0.at[at], xl.at[at], fr_send, xl_recv.at[q], (me, right)).start()
        remote(x0.at[at], xr.at[at], fl_send, xr_recv.at[q], (me, left)).start()

    def relay(q):
        at = pl.ds(4 * q, 4)
        lo = pl.ds(4 * q, 2)
        hi = pl.ds(4 * q + 2, 2)
        wait_bytes(xl.at[at], xl_recv.at[q])
        remote(xl.at[lo], xo.at[lo], rr_send, xoa_recv, (me, right)).start()
        wait_bytes(xr.at[at], xr_recv.at[q])
        remote(xr.at[hi], xo.at[hi], rl_send, xob_recv, (me, left)).start()

    wait_bytes(x0.at[pl.ds(2 * sib, 2)], sm_recv.at[p])
    forward(p)

    def forwards(g, _):
        q = chip_from(g)
        wait_bytes(x0.at[pl.ds(4 * q, 4)], sm_recv.at[q])
        forward(q)
        return 0

    lax.fori_loop(1, 16, forwards, 0)

    def relays(g, _):
        relay(chip_from(g))
        return 0

    def place_matrix(n, _):
        ri = n // 6
        o = lax.rem(n, 6)
        k = lax.broadcasted_iota(I32, (256, 256), 0)
        col = lax.broadcasted_iota(I32, (256, 256), 1)
        bb = (col & 63) - 8 * o
        hit = (k == 32 * ri + (col >> 6) * 24 + bb) & (bb >= 0) & (bb < 24)
        ebuf[n] = jnp.where(hit, 1.0, 0.0).astype(BF16)
        return 0

    lax.fori_loop(0, 24, place_matrix, 0)
    for o in (0, 1, 8, 9):
        mbuf[o] = jnp.zeros((256, KA), BF16)

    lax.fori_loop(0, 8, relays, 0)

    wait_bytes(rbuf.at[pl.ds(0, 31 * 16)], sr_recv)
    lane = lax.broadcasted_iota(I32, (8, 128), 1)
    rowi = lax.broadcasted_iota(I32, (8, 128), 0)
    pickrow = jnp.where(lane == rowi, 1.0, 0.0).astype(BF16)
    where = dot_nt(pickrow, rbuf[:, KW:KA]).astype(I32)
    blk = where[0:1]
    key = where[1:2] * 256 + (blk & 3) * 64 + (blk >> 2)

    def collect(o, _):
        rows = lax.broadcasted_iota(I32, (256, 512), 0) + o * 256
        pick = jnp.where(rows == key, 1.0, 0.0).astype(BF16)
        mbuf[o + 2] = dot(pick, rbuf[...]).astype(BF16)
        return 0

    lax.fori_loop(0, 6, collect, 0)

    lax.fori_loop(8, 16, relays, 0)

    def assemble(v, _):
        for c in range(2):
            for w in range(2):
                acc = None
                for d in range(3):
                    first = c * 576 + 96 * (w + 2 * d)
                    base = first // 128 * 128
                    ri = (first - base) // 32
                    term = dot(
                        mbuf[v - d + 2, :, base : base + 256],
                        ebuf[ri * 6 + jnp.clip(v - d, 0, 5)],
                    )
                    acc = term if acc is None else acc + term
                for a4 in range(4):
                    row = c * 64 + 8 * v + 4 * w + a4
                    at = pl.ds(pl.multiple_of(row * 64, 64), 64)
                    for h in range(2):
                        ks[h, at, :] = jnp.concatenate(
                            [
                                acc[j * 64 : j * 64 + 64, a4 * 64 : a4 * 64 + 64]
                                for j in (2 * h, 2 * h + 1)
                            ],
                            axis=1,
                        )
        return 0

    lax.fori_loop(0, 8, assemble, 0)

    def gather_rows(i, _):
        for h in range(2):
            lb[i, :, h * 128 : h * 128 + 128] = ks[h, pl.ds(i, 128, stride=64), :].astype(BF16)
        return 0

    lax.fori_loop(0, 64, gather_rows, 0)

    eye = jnp.where(
        lax.broadcasted_iota(I32, (128, 128), 0) == lax.broadcasted_iota(I32, (128, 128), 1), 1.0, 0.0
    ).astype(BF16)

    def transpose(ref, q):
        def one(g, _):
            part = ref[pl.ds(4 * g, 4)].reshape(256, COLS)
            xt[q * 128 : q * 128 + 128, pl.ds(pl.multiple_of(g * 256, 256), 256)] = dot_nt(eye, part).astype(BF16)
            return 0

        lax.fori_loop(0, 16, one, 0)

    def multiply(parts):
        def one(i, _):
            ids = [pat[4 * i + j] for j in range(4)]
            right_side = jnp.concatenate(
                [jnp.concatenate([ref[n] for n in ids], axis=0) for ref, _ in parts], axis=1
            )
            out = dot(lb[i], right_side).astype(BF16)
            at = pl.ds(pl.multiple_of(i * 64, 64), 64)
            for n, (_, q) in enumerate(parts):
                pb[q, at, 0:128] = out[0:64, n * 128 : n * 128 + 128]
                pb[q, at, 128:256] = out[64:128, n * 128 : n * 128 + 128]
            return 0

        lax.fori_loop(0, 64, one, 0)

    transpose(x0, 0)
    transpose(xl, 1)
    transpose(xr, 2)
    multiply([(x0, 0), (xl, 1)])
    lo = xo.at[pl.ds(0, 32)]
    wait_bytes(lo, xoa_recv)
    wait_bytes(lo, xob_recv)
    transpose(xo, 3)
    multiply([(xr, 2), (xo, 3)])

    order = (y, left, right, opp)
    for q in (1, 2, 3, 0):
        g = dot(xt[...], pb[q])
        for a in range(4):
            for b in range(8):
                at = pl.ds(pl.multiple_of(order[a] * 64 + (b // 2) * 16, 16), 16)
                gst[b % 2, q, at, :] = g[a * 128 + b * 16 : a * 128 + b * 16 + 16]
        remote(gst.at[1 - core, q], d0.at[q], d_send.at[q], d_recv.at[q], (sib, y)).start()

    targets = {1: (left, 2), 2: (right, 1), 3: (opp, 3)}
    for q in (1, 2, 3):
        wait_bytes(d0.at[q], d_recv.at[q])
        hs[q - 1] = (gst[core, q] + d0[q]).astype(BF16)
        dev, lands = targets[q]
        remote(hs.at[q - 1], hr.at[lands - 1], h_send.at[q - 1], h_recv.at[lands - 1], (me, dev)).start()
    wait_bytes(d0.at[0], d_recv.at[0])
    total = gst[core, 0] + d0[0]
    for q in (1, 2, 3):
        wait_bytes(hr.at[q - 1], h_recv.at[q - 1])
        total = total + hr[q - 1].astype(F32)
    tot[...] = total.reshape(16, 16, 256)

    def send_tot(g, _):
        q = chip_at(g)
        remote(tot.at[q], tr.at[p], t_send, t_recv, (q * 2 + core, y)).start()
        return 0

    lax.fori_loop(1, 16, send_tot, 0)
    tr[p] = tot[p]
    wait_bytes(tr.at[pl.ds(0, 15)], t_recv)
    final = jnp.sum(tr[...], axis=0)
    stiff[...] = final[:, 0:128]
    mass[...] = final[:, 128:256]

    wait_bytes(send_m.at[pl.ds(0, 62)], sm_send)
    wait_bytes(send_r.at[pl.ds(0, 31 * 16)], sr_send)
    wait_bytes(x0, fr_send)
    wait_bytes(x0, fl_send)
    wait_bytes(lo, rr_send)
    wait_bytes(lo, rl_send)
    for q in range(4):
        wait_bytes(d0.at[q], d_send.at[q])
    for q in range(3):
        wait_bytes(hs.at[q], h_send.at[q])
    wait_bytes(tot.at[pl.ds(0, 15)], t_send)


def body(elem_records, elem_owner, elem_block, elem_offset, modes, mode_readers, pattern):
    lane = lax.broadcasted_iota(I32, (256, 128), 1)
    place = jnp.where(
        lane == 0, elem_block[:, None], jnp.where(lane == 1, elem_offset[:, None], 0)
    ).astype(BF16)
    flat = mode_readers.reshape(-1)
    ids = jnp.arange(32, dtype=I32)
    rank = jnp.sum(((flat[:, None] == flat[None, :]) & (ids[:, None] < ids[None, :])).astype(I32), axis=0)
    slot = flat * 2 + rank
    hit = slot[None, :] == jnp.arange(NQ, dtype=I32)[:, None]
    midx = jnp.sum(jnp.where(hit, ids[None, :] // 2 + 1, 0), axis=1) - 1
    dma = pltpu.SemaphoreType.DMA
    vm = pl.BlockSpec(memory_space=pltpu.VMEM)
    sm = pl.BlockSpec(memory_space=pltpu.SMEM)
    xbuf = pltpu.VMEM((NQ, BS, COLS), BF16)
    return pl.pallas_call(
        kernel,
        out_shape=(jax.ShapeDtypeStruct((16, 128), F32), jax.ShapeDtypeStruct((16, 128), F32)),
        in_specs=[sm, sm, vm, vm, vm, vm, vm],
        out_specs=(vm, vm),
        scratch_shapes=[
            xbuf, xbuf, xbuf, xbuf, xbuf,
            pltpu.VMEM((512, KA), BF16),
            pltpu.VMEM((512, KA), BF16),
            pltpu.VMEM((24, 256, 256), BF16),
            pltpu.VMEM((10, 256, KA), BF16),
            pltpu.VMEM((2, 128 * 64, 128), F32),
            pltpu.VMEM((64, 128, 256), BF16),
            pltpu.VMEM((512, 4096), BF16),
            pltpu.VMEM((4, 4096, 256), BF16),
            pltpu.VMEM((2, 4, 256, 256), F32),
            pltpu.VMEM((4, 256, 256), F32),
            pltpu.VMEM((3, 256, 256), BF16),
            pltpu.VMEM((3, 256, 256), BF16),
            pltpu.VMEM((16, 16, 256), F32),
            pltpu.VMEM((16, 16, 256), F32),
            dma, dma((16,)), dma, dma, dma, dma, dma((16,)), dma((16,)),
            dma, dma, dma, dma, dma((4,)), dma((4,)), dma((3,)), dma((3,)), dma, dma,
        ],
        compiler_params=pltpu.CompilerParams(
            collective_id=0, has_side_effects=True, vmem_limit_bytes=60 << 20
        ),
        name="sweep",
    )(midx, pattern.reshape(-1), elem_records, place, elem_owner.reshape(1, 256), elem_owner, modes)


def solution(mesh):
    in_specs = (
        P(("sub", "col"), None),
        P(("sub", "col"), None),
        P(("sub", "col")),
        P(("sub", "col")),
        P("sub", None, "col"),
        P("sub", None),
        P("sub", None),
    )
    out_specs = (P("sub", "col"), P("sub", "col"))
    return jax.shard_map(body, mesh=mesh, in_specs=in_specs, out_specs=out_specs, check_vma=False)
```

time: 365 us -> 126 us (0.35)
  Pallas kernels: 0 us -> 118 us
  local copies, waits for them, and re-layouts: 119 us -> 4.39 us
  waiting for transfers between devices: 110 us -> 0 us
  blocking collectives: 60.3 us -> 0 us
  other arithmetic: 45.7 us -> 1.47 us
  between operations: 14 us -> 0.69 us
  matrix products: 11 us -> 0 us
  starting transfers between devices: 4.01 us -> 0 us
    pallas_call x0 -> x1, Pallas kernels: none -> 118 us  [body(): pl.pallas_call(kernel, out_shape=(jax.ShapeDtypeStruct((16, 128), F32), j...]
    psum x1 -> x0, waiting for transfers between devices: 102 us -> none  [body(): gram_total = lax.psum(gram_term, 'sub')]
    all_to_all x2 -> x0, blocking collectives: 49 us -> none  [the longest x1 28.2 us: body(): lax.all_to_all(send_records.reshape(sub_count, elem_slots, KW), 'sub', sp...]
    scatter-add x6 -> x0, other arithmetic: 36.5 us -> none  [the longest x1 23.6 us: assemble(): summed = jnp.zeros((block_total * 6, KW), jnp.float32).at[row_ids].add(al...]
    unnamed x23 -> x17, local copies, waits for them, and re-layouts: 34.2 us -> 3.63 us
    reshape x3 -> x2, local copies, waits for them, and re-layouts: 28.2 us -> 0.76 us  [the longest x1 0.67 us: body(): pattern.reshape(-1)]
    slice x1 -> x0, local copies, waits for them, and re-layouts: 25.8 us -> none  [assemble(): piece = jnp.transpose(summed[:, offset_step], (1, 0, 2, 3))]
    convert_element_type x2 -> x0, local copies, waits for them, and re-layouts: 13.1 us -> none  [the longest x1 13 us: assemble(): return result.reshape(2, NQ, NNZ, BS, BS).astype(jnp.bfloat16)]
  transfers between devices with their start and end apart: 4 -> 0, of which waited for: 2 -> 0; matrix products, arithmetic and copies ran while one was open for 45% -> 0% of each run, Pallas kernels for 0% -> 0%
where the time goes in v1:
time: 126 us; the launch traced here: 125 us
  Pallas kernels  118 us (94%)
  local copies, waits for them, and re-layouts  4.39 us (3%)
  other arithmetic  1.47 us (1%)
    pallas_call x1, Pallas kernels, body(): pl.pallas_call(kernel, out_shape=(jax.ShapeDtypeStruct((16, 128), F32), j...  118 us
    unnamed x17, local copies, waits for them, and re-layouts  3.63 us

profile of v1, /device:TPU:1, one launch (start us, length us, event | category | flops | bytes accessed | tf_op | source)
XLA Modules:
  0.0 124.7 jit_solution(184702075817358371)
XLA Ops:
  0.6 0.0 copy-start.5
  0.7 0.7 copy-done.5
  1.3 0.1 copy.14
  1.4 0.1 reshape.64
  1.5 0.1 convert_reduce_fusion
  1.6 0.0 copy-start.2
  1.6 0.1 select_reduce_fusion
  1.7 0.5 broadcast_add_fusion.midx
  2.2 0.1 copy-done.2
  2.3 0.1 copy.15
  2.4 0.0 copy-start.3
  2.4 0.0 copy-start.4
  2.4 0.7 reshape.65.pat
  3.1 0.0 copy-done.3
  3.1 0.0 copy-done.4
  3.1 0.0 copy-start.1
  3.1 0.8 select_convert_fusion.place
  3.8 0.0 copy-done.1
  3.8 0.8 copy.16.owner_col
  4.6 118.1 %sweep.1 = (f32[16,128]{1,0:T(8,128)}, f32[16,128]{1,0:T(8,128)}) custom-call(s32[64]{0:T(128)} %broadcast_add_fusion.midx, s32[256]{0:T(256)} %reshape.65.pat, bf16[256,1152]{1,0:T(8,128)(2,1)} %rec.1, bf16[256,128]{1,0:T(8,128)(2,1)} %select_convert_fusion.place, s32[1,256]{1,0:T(1,128)} %bitcast.1, s32[256,1]{1,0:T(8,128)} %copy.16.owner_col, ...), custom_call_target="tpu_custom_call" | custom-call | tf_op jit(solution)/shard_map/sweep/pallas_call | solution.py:333
  122.7 0.0 copy-start
  122.8 1.3 %copy.19 = f32[16,128]{1,0:T(8,128)} copy(f32[16,128]{1,0:T(8,128)} %get-tuple-element.8) | data formatting | bytes 16384
  124.1 0.0 copy-done
  124.1 0.6 copy.20
  (2 shorter events, 0.0 us)
Async XLA Ops:
  0.6 0.7 copy-start.5
  1.6 0.7 copy-start.2
  2.4 0.7 copy-start.3
  2.4 0.7 copy-start.4
  3.1 0.8 copy-start.1
  122.7 1.3 %copy-start = (f32[16,128]{1,0:T(8,128)S(1)}, f32[16,128]{1,0:T(8,128)}, u32[]{:S(2)}) copy-start(f32[16,128]{1,0:T(8,128)} %get-tuple-element.9) | copy-start | bytes 24580

commit v2 on v1

v2 whole, which is shorter than its diff:
```python
import functools

import jax
import jax.numpy as jnp
from jax import lax
from jax.experimental import pallas as pl
from jax.experimental.pallas import tpu as pltpu
from jax.sharding import PartitionSpec as P

MESH = pl.DeviceIdType.MESH
BF16 = jnp.bfloat16
F32 = jnp.float32
I32 = jnp.int32

BS = 64
NQ = 64
NNZ = 4
KW = 1152
KA = 1280
COLS = 128
SLOTS_E = 16


def dot(a, b):
    return jnp.dot(a, b, preferred_element_type=F32)


def dot_nt(a, b):
    return lax.dot_general(a, b, (((1,), (1,)), ((), ())), preferred_element_type=F32)


FAR = (
    (2, 2), (2, 0), (0, 2), (3, 2), (2, 3), (1, 2), (2, 1), (3, 1),
    (1, 3), (3, 3), (1, 1), (3, 0), (0, 3), (1, 0), (0, 1),
)


def kernel(
    midx, pat, rec, place, owner_row, owner_col, modes,
    stiff, mass,
    send_m, xf, send_r, rbuf, ebuf, mbuf, ks, lb, xt, pb, gst, d0, hs, hr, tot, tr,
    sm_send, a_recv, r_send, r_recv, w_send, w_recv, b_send, b_recv, c_send, c_recv,
    e_send, e_recv, d_send, d_recv, h_send, h_recv, t_send, t_recv, patv, pats, p_send, p_recv, p_copy,
):
    me = lax.axis_index("sub")
    y = lax.axis_index("col")
    core = lax.rem(me, 2)
    p = me // 2
    z = p // 4
    x = lax.rem(p, 4)
    sib = p * 2 + 1 - core
    host = y // 2
    guest = lax.rem(core + host, 2)
    own = 4 * guest
    y1 = y + 1 - 2 * lax.rem(y, 2)
    y3 = 3 - y
    y2 = 3 - y1
    order = (y, y1, y3, y2)

    def chip_at(dz, dx):
        return lax.rem(z + dz, 4) * 4 + lax.rem(x + dx, 4)

    def remote(src, dst, ssem, rsem, dev):
        return pltpu.make_async_remote_copy(
            src_ref=src, dst_ref=dst, send_sem=ssem, recv_sem=rsem, device_id=dev, device_id_type=MESH
        )

    def wait_bytes(ref, sem):
        pltpu.make_async_copy(ref, ref, sem).wait()

    barrier = pltpu.get_barrier_semaphore()

    def hello(dev):
        pl.semaphore_signal(barrier, inc=1, device_id=dev, device_id_type=MESH)

    hello((sib, y))
    for yy in order[1:]:
        for cc in range(2):
            hello((p * 2 + cc, yy))

    def greet(g, _):
        q = chip_at(g // 4, lax.rem(g, 4))
        for cc in range(2):
            hello((q * 2 + cc, y))
        return 0

    lax.fori_loop(1, 16, greet, 0)

    @pl.when(guest == 1)
    def _():
        def greet_far(g, _):
            hello((g, y3))
            return 0

        lax.fori_loop(0, 32, greet_far, 0)

    def fill(s, _):
        k = midx[s]
        block = modes[jnp.maximum(k, 0)]
        send_m[s] = jnp.where(k >= 0, block, jnp.zeros_like(block))
        return 0

    lax.fori_loop(0, NQ, fill, 0, unroll=4)

    before = lax.broadcasted_iota(I32, (256, 256), 0) < lax.broadcasted_iota(I32, (256, 256), 1)
    same = owner_col[...] == owner_row[...]
    rank = jnp.sum(jnp.where(same & before, 1, 0), axis=0, keepdims=True)
    pos = owner_row[...] * SLOTS_E + rank

    def permute(g, _):
        rows = lax.broadcasted_iota(I32, (128, 256), 0) + g * 128
        pick = jnp.where(rows == pos, 1.0, 0.0).astype(BF16)
        at = pl.ds(pl.multiple_of(g * 128, 128), 128)
        send_r[at, 0:KW] = dot(pick, rec[...]).astype(BF16)
        send_r[at, KW:KA] = dot(pick, place[...]).astype(BF16)
        return 0

    lax.fori_loop(0, 4, permute, 0)

    pl.semaphore_wait(barrier, 53)

    xf[own, pl.ds(2 * me, 2)] = send_m[pl.ds(2 * me, 2)]

    @pl.when(guest == 0)
    def _():
        away = remote(pat, patv, p_send, p_recv, (sib, y))
        away.start()
        here = pltpu.make_async_copy(pat, pats, p_copy)
        here.start()
        away.wait_send()
        here.wait()

    def other(cc):
        return lax.rem(cc + host, 2)

    def send_mode(dest, lands):
        remote(
            send_m.at[pl.ds(2 * dest, 2)], xf.at[lands, pl.ds(2 * me, 2)], sm_send, a_recv.at[p], (dest, y)
        ).start()

    def rows16(n):
        return pl.ds(pl.multiple_of(n * 16, 16), 16)

    def send_rec(q, cc):
        far = other(cc)
        remote(
            send_r.at[rows16(q * 2 + cc)], rbuf.at[rows16(32 * far + me)], r_send, r_recv,
            (q * 2 + host, y + far * (y3 - y)),
        ).start()

    send_mode(sib, 4 * (1 - guest))
    for dz, dx in FAR:
        q = chip_at(dz, dx)
        for cc in range(2):
            send_mode(q * 2 + cc, 4 * other(cc))

    @pl.when(guest == 0)
    def _():
        rbuf[rows16(me)] = send_r[rows16(me)]

    for dz, dx in FAR:
        q = chip_at(dz, dx)
        for cc in range(2):
            send_rec(q, cc)
    remote(
        send_r.at[rows16(p * 2 + 1 - host)], rbuf.at[rows16(32 + me)], r_send, r_recv, (p * 2 + host, y3)
    ).start()

    @pl.when(guest == 1)
    def _():
        remote(send_r.at[rows16(sib)], rbuf.at[rows16(me)], r_send, r_recv, (sib, y)).start()

    def first(q, fresh):
        at = pl.ds(4 * q, 4)
        wait_bytes(fresh, a_recv.at[q])
        remote(
            xf.at[own, at], xf.at[1 + guest, at], b_send, b_recv.at[q],
            (me + guest * (sib - me), y1 + guest * (y3 - y1)),
        ).start()

        @pl.when(guest == 0)
        def _():
            remote(xf.at[0, at], xf.at[0, at], c_send, c_recv.at[0], (sib, y)).start()

    def second(q):
        at = pl.ds(4 * q, 4)
        wait_bytes(xf.at[1 + guest, at], b_recv.at[q])

        @pl.when(guest == 1)
        def _():
            remote(xf.at[2, at], xf.at[3, at], e_send, e_recv.at[q], (me, y1)).start()

        remote(xf.at[1 + guest, at], xf.at[1 + guest, at], c_send, c_recv.at[1 + guest], (sib, y)).start()

    def third(q):
        at = pl.ds(4 * q, 4)

        @pl.when(guest == 1)
        def _():
            wait_bytes(xf.at[3, at], e_recv.at[q])
            remote(xf.at[3, at], xf.at[3, at], c_send, c_recv.at[3], (sib, y)).start()

    chips = [p] + [chip_at((4 - dz) % 4, (4 - dx) % 4) for dz, dx in FAR]
    for n, q in enumerate(chips):
        first(q, xf.at[own, pl.ds(2 * sib, 2)] if n == 0 else xf.at[own, pl.ds(4 * q, 4)])

    def place_matrix(n, _):
        ri = n // 6
        o = lax.rem(n, 6)
        k = lax.broadcasted_iota(I32, (256, 256), 0)
        col = lax.broadcasted_iota(I32, (256, 256), 1)
        bb = (col & 63) - 8 * o
        hit = (k == 32 * ri + (col >> 6) * 24 + bb) & (bb >= 0) & (bb < 24)
        ebuf[n] = jnp.where(hit, 1.0, 0.0).astype(BF16)
        return 0

    lax.fori_loop(0, 24, place_matrix, 0)
    for o in (0, 1, 8, 9):
        mbuf[o] = jnp.zeros((128, KA), BF16)

    for q in chips:
        second(q)
    for q in chips:
        third(q)

    @pl.when(guest == 1)
    def _():
        wait_bytes(patv, p_recv)
        here = pltpu.make_async_copy(patv, pats, p_copy)
        here.start()
        here.wait()

    @pl.when(guest == 0)
    def _():
        wait_bytes(rbuf.at[pl.ds(0, 31 * 16)], r_recv)

    @pl.when(guest == 1)
    def _():
        wait_bytes(rbuf.at[pl.ds(0, 32 * 16)], r_recv)

    mine = pl.ds(pl.multiple_of(512 * guest, 512), 512)
    remote(rbuf.at[mine], rbuf.at[mine], w_send, w_recv, (sib, y)).start()
    wait_bytes(rbuf.at[pl.ds(pl.multiple_of(512 * (1 - guest), 512), 512)], w_recv)

    lane = lax.broadcasted_iota(I32, (8, 128), 1)
    rowi = lax.broadcasted_iota(I32, (8, 128), 0)
    pickrow = jnp.where(lane == rowi, 1.0, 0.0).astype(BF16)
    where = dot_nt(pickrow, rbuf[:, KW:KA]).astype(I32)
    blk = where[0:1]
    row = (blk >> 2) - 32 * core
    key = jnp.where((row >= 0) & (row < 32), where[1:2] * 128 + (blk & 3) * 32 + row, -1)

    def collect(o, _):
        rows = lax.broadcasted_iota(I32, (128, 1024), 0) + o * 128
        pick = jnp.where(rows == key, 1.0, 0.0).astype(BF16)
        mbuf[o + 2] = dot(pick, rbuf[...]).astype(BF16)
        return 0

    lax.fori_loop(0, 6, collect, 0)

    def assemble(v, _):
        for c in range(2):
            for w in range(2):
                acc = None
                for d in range(3):
                    start = c * 576 + 96 * (w + 2 * d)
                    base = start // 128 * 128
                    ri = (start - base) // 32
                    term = dot(
                        mbuf[v - d + 2, :, base : base + 256],
                        ebuf[ri * 6 + jnp.clip(v - d, 0, 5)],
                    )
                    acc = term if acc is None else acc + term
                acc = acc.astype(BF16)
                for a4 in range(4):
                    ks[c * 64 + 8 * v + 4 * w + a4] = jnp.concatenate(
                        [acc[j * 32 : j * 32 + 32, a4 * 64 : a4 * 64 + 64] for j in range(4)], axis=1
                    )
        return 0

    lax.fori_loop(0, 8, assemble, 0)

    r0 = lax.broadcasted_iota(I32, (256, 256), 0)
    r1 = lax.broadcasted_iota(I32, (256, 256), 1)
    swap = jnp.where((r0 >> 4 == (r1 & 15)) & ((r0 & 15) == r1 >> 4), 1.0, 0.0).astype(BF16)

    def turn(n, _):
        arow = pl.ds(pl.multiple_of(n // 2 * 16, 16), 16)
        irow = pl.ds(pl.multiple_of(lax.rem(n, 2) * 16, 16), 16)
        part = ks[arow, irow, :].reshape(256, 256)
        lb[irow, arow, :] = dot(swap, part).astype(BF16).reshape(16, 16, 256)
        return 0

    lax.fori_loop(0, 16, turn, 0, unroll=2)

    eye = jnp.where(
        lax.broadcasted_iota(I32, (128, 128), 0) == lax.broadcasted_iota(I32, (128, 128), 1), 1.0, 0.0
    ).astype(BF16)

    def transpose(k):
        def one(g, _):
            part = xf[k, pl.ds(32 * core + 4 * g, 4)].reshape(256, COLS)
            xt[k * 128 : k * 128 + 128, pl.ds(pl.multiple_of(g * 256, 256), 256)] = dot_nt(eye, part).astype(BF16)
            return 0

        lax.fori_loop(0, 8, one, 0, unroll=4)

    def multiply(kinds):
        def one(i, _):
            ids = [pats[core, 4 * i + j] for j in range(4)]
            right_side = jnp.concatenate(
                [jnp.concatenate([xf[k, n] for n in ids], axis=0) for k in kinds], axis=1
            )
            out = dot(lb[i], right_side).astype(BF16)
            at = pl.ds(pl.multiple_of(i * 64, 64), 64)
            for n, k in enumerate(kinds):
                pb[k, at, 0:128] = out[0:64, n * 128 : n * 128 + 128]
                pb[k, at, 128:256] = out[64:128, n * 128 : n * 128 + 128]
            return 0

        lax.fori_loop(0, 32, one, 0, unroll=4)

    @pl.when(guest == 0)
    def _():
        wait_bytes(xf.at[2], c_recv.at[2])
        wait_bytes(xf.at[3], c_recv.at[3])

    @pl.when(guest == 1)
    def _():
        wait_bytes(xf.at[0], c_recv.at[0])
        wait_bytes(xf.at[1], c_recv.at[1])

    for k in range(4):
        transpose(k)
    multiply((0, 1))
    multiply((2, 3))

    for q in (3, 2, 1, 0):
        g = dot(xt[...], pb[q])
        for a in range(4):
            for b in range(8):
                at = pl.ds(pl.multiple_of(order[a] * 64 + (b // 2) * 16, 16), 16)
                gst[b % 2, q, at, :] = g[a * 128 + b * 16 : a * 128 + b * 16 + 16]
        remote(gst.at[1 - core, q], d0.at[q], d_send.at[q], d_recv.at[q], (sib, y)).start()

    for q in (3, 2, 1):
        wait_bytes(d0.at[q], d_recv.at[q])
        hs[q - 1] = (gst[core, q] + d0[q]).astype(BF16)
        remote(hs.at[q - 1], hr.at[y], h_send.at[q - 1], h_recv.at[y], (me, order[q])).start()
    wait_bytes(d0.at[0], d_recv.at[0])
    total = gst[core, 0] + d0[0]
    for yy in (y2, y3, y1):
        wait_bytes(hr.at[yy], h_recv.at[yy])
        total = total + hr[yy].astype(F32)
    tot[...] = total.reshape(16, 16, 256)

    for dz, dx in FAR:
        q = chip_at(dz, dx)
        remote(tot.at[q], tr.at[p], t_send, t_recv, (q * 2 + core, y)).start()
    tr[p] = tot[p]
    wait_bytes(tr.at[pl.ds(0, 15)], t_recv)
    final = jnp.sum(tr[...], axis=0)
    stiff[...] = final[:, 0:128]
    mass[...] = final[:, 128:256]

    wait_bytes(send_m.at[pl.ds(0, 62)], sm_send)
    wait_bytes(rbuf.at[mine], w_send)
    wait_bytes(xf.at[0], b_send)
    wait_bytes(xf.at[pl.ds(0, 2)], c_send)

    @pl.when(guest == 0)
    def _():
        wait_bytes(send_r.at[pl.ds(0, 31 * 16)], r_send)

    @pl.when(guest == 1)
    def _():
        wait_bytes(send_r, r_send)
        wait_bytes(xf.at[0], e_send)

    for q in range(4):
        wait_bytes(d0.at[q], d_send.at[q])
    for q in range(3):
        wait_bytes(hs.at[q], h_send.at[q])
    wait_bytes(tot.at[pl.ds(0, 15)], t_send)


def body(elem_records, elem_owner, elem_block, elem_offset, modes, mode_readers, pattern):
    lane = lax.broadcasted_iota(I32, (256, 128), 1)
    place = jnp.where(
        lane == 0, elem_block[:, None], jnp.where(lane == 1, elem_offset[:, None], 0)
    ).astype(BF16)
    flat = mode_readers.reshape(-1)
    ids = jnp.arange(32, dtype=I32)
    rank = jnp.sum(((flat[:, None] == flat[None, :]) & (ids[:, None] < ids[None, :])).astype(I32), axis=0)
    slot = flat * 2 + rank
    hit = slot[None, :] == jnp.arange(NQ, dtype=I32)[:, None]
    midx = jnp.sum(jnp.where(hit, ids[None, :] // 2 + 1, 0), axis=1) - 1
    dma = pltpu.SemaphoreType.DMA
    vm = pl.BlockSpec(memory_space=pltpu.VMEM)
    sm = pl.BlockSpec(memory_space=pltpu.SMEM)
    return pl.pallas_call(
        kernel,
        out_shape=(jax.ShapeDtypeStruct((16, 128), F32), jax.ShapeDtypeStruct((16, 128), F32)),
        in_specs=[sm, vm, vm, vm, vm, vm, vm],
        out_specs=(vm, vm),
        scratch_shapes=[
            pltpu.VMEM((NQ, BS, COLS), BF16),
            pltpu.VMEM((5, NQ, BS, COLS), BF16),
            pltpu.VMEM((512, KA), BF16),
            pltpu.VMEM((1024, KA), BF16),
            pltpu.VMEM((24, 256, 256), BF16),
            pltpu.VMEM((10, 128, KA), BF16),
            pltpu.VMEM((128, 32, 256), BF16),
            pltpu.VMEM((32, 128, 256), BF16),
            pltpu.VMEM((512, 2048), BF16),
            pltpu.VMEM((4, 2048, 256), BF16),
            pltpu.VMEM((2, 4, 256, 256), F32),
            pltpu.VMEM((4, 256, 256), F32),
            pltpu.VMEM((3, 256, 256), BF16),
            pltpu.VMEM((4, 256, 256), BF16),
            pltpu.VMEM((16, 16, 256), F32),
            pltpu.VMEM((16, 16, 256), F32),
            dma, dma((16,)), dma, dma, dma, dma, dma, dma((16,)), dma, dma((4,)),
            dma, dma((16,)), dma((4,)), dma((4,)), dma((3,)), dma((4,)), dma, dma,
            pltpu.VMEM((2, 128), I32), pltpu.SMEM((2, 128), I32), dma, dma, dma,
        ],
        compiler_params=pltpu.CompilerParams(
            collective_id=0, has_side_effects=True, vmem_limit_bytes=60 << 20
        ),
        name="sweep",
    )(midx, pattern.reshape(2, 128), elem_records, place, elem_owner.reshape(1, 256), elem_owner, modes)


def solution(mesh):
    in_specs = (
        P(("sub", "col"), None),
        P(("sub", "col"), None),
        P(("sub", "col")),
        P(("sub", "col")),
        P("sub", None, "col"),
        P("sub", None),
        P("sub", None),
    )
    out_specs = (P("sub", "col"), P("sub", "col"))
    return jax.shard_map(body, mesh=mesh, in_specs=in_specs, out_specs=out_specs, check_vma=False)
```

time: 126 us -> 95.1 us (0.75)
  Pallas kernels: 118 us -> 88.4 us
    pallas_call x1, Pallas kernels: 118 us -> 88.4 us  [body(): pl.pallas_call(kernel, out_shape=(jax.ShapeDtypeStruct((16, 128), F32), j...]
where the time goes in v2:
time: 95.1 us; the launch traced here: 94.9 us
  Pallas kernels  88.4 us (93%)
  local copies, waits for them, and re-layouts  4.39 us (5%)
  other arithmetic  1.47 us (2%)
    pallas_call x1, Pallas kernels, body(): pl.pallas_call(kernel, out_shape=(jax.ShapeDtypeStruct((16, 128), F32), j...  88.4 us
    unnamed x17, local copies, waits for them, and re-layouts  3.63 us

profile of v2, /device:TPU:1, one launch (start us, length us, event | category | flops | bytes accessed | tf_op | source)
XLA Modules:
  0.0 94.9 jit_solution(4609762007712080105)
XLA Ops:
  0.6 0.0 copy-start.5
  0.7 0.7 copy-done.5
  1.3 0.1 copy.15
  1.4 0.1 reshape.64
  1.5 0.1 convert_reduce_fusion
  1.6 0.0 copy-start.2
  1.6 0.1 select_reduce_fusion
  1.7 0.5 broadcast_add_fusion.midx
  2.2 0.1 copy-done.2
  2.3 0.1 copy.16
  2.4 0.0 copy-start.3
  2.4 0.0 copy-start.4
  2.4 0.7 reshape.65.pat
  3.1 0.0 copy-done.3
  3.1 0.0 copy-done.4
  3.1 0.0 copy-start.1
  3.1 0.8 select_convert_fusion.place
  3.8 0.0 copy-done.1
  3.8 0.8 copy.17.owner_col
  4.6 88.4 %sweep.1 = (f32[16,128]{1,0:T(8,128)}, f32[16,128]{1,0:T(8,128)}) custom-call(s32[64]{0:T(128)} %broadcast_add_fusion.midx, s32[2,128]{1,0:T(2,128)} %reshape.65.pat, bf16[256,1152]{1,0:T(8,128)(2,1)} %rec.1, bf16[256,128]{1,0:T(8,128)(2,1)} %select_convert_fusion.place, s32[1,256]{1,0:T(1,128)} %bitcast.1, s32[256,1]{1,0:T(8,128)} %copy.17.owner_col, ...), custom_call_target="tpu_custom_call" | custom-call | tf_op jit(solution)/shard_map/sweep/pallas_call | solution.py:401
  93.0 0.0 copy-start
  93.0 1.3 %copy.20 = f32[16,128]{1,0:T(8,128)} copy(f32[16,128]{1,0:T(8,128)} %get-tuple-element.8) | data formatting | bytes 16384
  94.3 0.0 copy-done
  94.3 0.6 copy.21
  (2 shorter events, 0.0 us)
Async XLA Ops:
  0.6 0.7 copy-start.5
  1.6 0.7 copy-start.2
  2.4 0.7 copy-start.3
  2.4 0.7 copy-start.4
  3.1 0.8 copy-start.1
  93.0 1.3 %copy-start = (f32[16,128]{1,0:T(8,128)S(1)}, f32[16,128]{1,0:T(8,128)}, u32[]{:S(2)}) copy-start(f32[16,128]{1,0:T(8,128)} %get-tuple-element.9) | copy-start | bytes 24580

commit v3 on v2

--- a/solution.py
+++ b/solution.py
@@ -36,11 +36,11 @@
 
 
 def kernel(
-    midx, pat, rec, place, owner_row, owner_col, modes,
-    stiff, mass,
+    pat, rec, owner_row, block_row, offset_row, modes, readers,
+    out,
     send_m, xf, send_r, rbuf, ebuf, mbuf, ks, lb, xt, pb, gst, d0, hs, hr, tot, tr,
     sm_send, a_recv, r_send, r_recv, w_send, w_recv, b_send, b_recv, c_send, c_recv,
-    e_send, e_recv, d_send, d_recv, h_send, h_recv, t_send, t_recv, patv, pats, p_send, p_recv, p_copy,
+    e_send, e_recv, d_send, d_recv, h_send, h_recv, t_send, t_recv, tab, patv, pats, mids, p_send, p_recv, p_copy, m_copy,
 ):
     me = lax.axis_index("sub")
     y = lax.axis_index("col")
@@ -94,38 +94,65 @@
 
         lax.fori_loop(0, 32, greet_far, 0)
 
-    def fill(s, _):
-        k = midx[s]
-        block = modes[jnp.maximum(k, 0)]
-        send_m[s] = jnp.where(k >= 0, block, jnp.zeros_like(block))
-        return 0
-
-    lax.fori_loop(0, NQ, fill, 0, unroll=4)
-
-    before = lax.broadcasted_iota(I32, (256, 256), 0) < lax.broadcasted_iota(I32, (256, 256), 1)
-    same = owner_col[...] == owner_row[...]
+    def iota(shape, axis):
+        return lax.broadcasted_iota(I32, shape, axis)
+
+    def eye(n):
+        return jnp.where(iota((n, n), 0) == iota((n, n), 1), 1.0, 0.0).astype(BF16)
+
+    named = dot_nt(eye(16), readers[...].astype(F32).astype(BF16))
+    subs = iota((16, 32), 1).astype(F32)
+    occurs = jnp.where((named[:, 0:1] == subs) | (named[:, 1:2] == subs), 1.0, 0.0)
+    lower = jnp.where(iota((16, 16), 0) > iota((16, 16), 1), 1.0, 0.0).astype(BF16)
+    ahead = dot(lower, occurs.astype(BF16))
+    number = (iota((16, 32), 0) + 1).astype(F32)
+    tab[...] = jnp.zeros((8, 128), I32)
+    tab[0:4, 0:64] = pat[...]
+    for n in range(2):
+        picked = jnp.sum(jnp.where((occurs > 0) & (ahead == n), number, 0.0), axis=0, keepdims=True)
+        tab[4 + n : 5 + n, 0:32] = picked.astype(I32) - 1
+    to_mids = pltpu.make_async_copy(tab, mids, m_copy)
+    to_mids.start()
+
+    lines = iota((128, 256), 0)
+    facts = jnp.where(
+        lines == 0, block_row[...], jnp.where(lines == 1, offset_row[...], jnp.where(lines == 2, owner_row[...], 0))
+    ).astype(F32).astype(BF16)
+    place = dot_nt(eye(256), facts)
+    before = iota((256, 256), 0) < iota((256, 256), 1)
+    same = place[:, 2:3] == owner_row[...].astype(F32)
     rank = jnp.sum(jnp.where(same & before, 1, 0), axis=0, keepdims=True)
     pos = owner_row[...] * SLOTS_E + rank
+    place = place.astype(BF16)
 
     def permute(g, _):
-        rows = lax.broadcasted_iota(I32, (128, 256), 0) + g * 128
-        pick = jnp.where(rows == pos, 1.0, 0.0).astype(BF16)
+        pick = jnp.where(iota((128, 256), 0) + g * 128 == pos, 1.0, 0.0).astype(BF16)
         at = pl.ds(pl.multiple_of(g * 128, 128), 128)
         send_r[at, 0:KW] = dot(pick, rec[...]).astype(BF16)
-        send_r[at, KW:KA] = dot(pick, place[...]).astype(BF16)
+        send_r[at, KW:KA] = dot(pick, place).astype(BF16)
         return 0
 
     lax.fori_loop(0, 4, permute, 0)
 
+    to_mids.wait()
+
+    def fill(s, _):
+        k = mids[4 + lax.rem(s, 2), s // 2]
+        block = modes[jnp.clip(k, 0, modes.shape[0] - 1)]
+        send_m[s] = jnp.where(k >= 0, block, jnp.zeros_like(block))
+        return 0
+
+    lax.fori_loop(0, NQ, fill, 0, unroll=4)
+
     pl.semaphore_wait(barrier, 53)
 
     xf[own, pl.ds(2 * me, 2)] = send_m[pl.ds(2 * me, 2)]
 
     @pl.when(guest == 0)
     def _():
-        away = remote(pat, patv, p_send, p_recv, (sib, y))
+        away = remote(tab, patv, p_send, p_recv, (sib, y))
         away.start()
-        here = pltpu.make_async_copy(pat, pats, p_copy)
+        here = pltpu.make_async_copy(tab, pats, p_copy)
         here.start()
         away.wait_send()
         here.wait()
@@ -158,10 +185,6 @@
     def _():
         rbuf[rows16(me)] = send_r[rows16(me)]
 
-    for dz, dx in FAR:
-        q = chip_at(dz, dx)
-        for cc in range(2):
-            send_rec(q, cc)
     remote(
         send_r.at[rows16(p * 2 + 1 - host)], rbuf.at[rows16(32 + me)], r_send, r_recv, (p * 2 + host, y3)
     ).start()
@@ -203,6 +226,9 @@
     chips = [p] + [chip_at((4 - dz) % 4, (4 - dx) % 4) for dz, dx in FAR]
     for n, q in enumerate(chips):
         first(q, xf.at[own, pl.ds(2 * sib, 2)] if n == 0 else xf.at[own, pl.ds(4 * q, 4)])
+    for dz, dx in FAR:
+        for cc in range(2):
+            send_rec(chip_at(dz, dx), cc)
 
     def place_matrix(n, _):
         ri = n // 6
@@ -229,6 +255,29 @@
         here = pltpu.make_async_copy(patv, pats, p_copy)
         here.start()
         here.wait()
+
+    turned = eye(128)
+
+    def transpose(k):
+        def one(g, _):
+            part = xf[k, pl.ds(32 * core + 4 * g, 4)].reshape(256, COLS)
+            xt[k * 128 : k * 128 + 128, pl.ds(pl.multiple_of(g * 256, 256), 256)] = dot_nt(turned, part).astype(BF16)
+            return 0
+
+        lax.fori_loop(0, 8, one, 0, unroll=4)
+
+    @pl.when(guest == 0)
+    def _():
+        wait_bytes(xf.at[2], c_recv.at[2])
+        wait_bytes(xf.at[3], c_recv.at[3])
+
+    @pl.when(guest == 1)
+    def _():
+        wait_bytes(xf.at[0], c_recv.at[0])
+        wait_bytes(xf.at[1], c_recv.at[1])
+
+    for k in range(4):
+        transpose(k)
 
     @pl.when(guest == 0)
     def _():
@@ -293,21 +342,9 @@
 
     lax.fori_loop(0, 16, turn, 0, unroll=2)
 
-    eye = jnp.where(
-        lax.broadcasted_iota(I32, (128, 128), 0) == lax.broadcasted_iota(I32, (128, 128), 1), 1.0, 0.0
-    ).astype(BF16)
-
-    def transpose(k):
-        def one(g, _):
-            part = xf[k, pl.ds(32 * core + 4 * g, 4)].reshape(256, COLS)
-            xt[k * 128 : k * 128 + 128, pl.ds(pl.multiple_of(g * 256, 256), 256)] = dot_nt(eye, part).astype(BF16)
-            return 0
-
-        lax.fori_loop(0, 8, one, 0, unroll=4)
-
     def multiply(kinds):
         def one(i, _):
-            ids = [pats[core, 4 * i + j] for j in range(4)]
+            ids = [pats[j, 32 * core + i] for j in range(4)]
             right_side = jnp.concatenate(
                 [jnp.concatenate([xf[k, n] for n in ids], axis=0) for k in kinds], axis=1
             )
@@ -320,22 +357,7 @@
 
         lax.fori_loop(0, 32, one, 0, unroll=4)
 
-    @pl.when(guest == 0)
-    def _():
-        wait_bytes(xf.at[2], c_recv.at[2])
-        wait_bytes(xf.at[3], c_recv.at[3])
-
-    @pl.when(guest == 1)
-    def _():
-        wait_bytes(xf.at[0], c_recv.at[0])
-        wait_bytes(xf.at[1], c_recv.at[1])
-
-    for k in range(4):
-        transpose(k)
-    multiply((0, 1))
-    multiply((2, 3))
-
-    for q in (3, 2, 1, 0):
+    def gram(q):
         g = dot(xt[...], pb[q])
         for a in range(4):
             for b in range(8):
@@ -343,10 +365,20 @@
                 gst[b % 2, q, at, :] = g[a * 128 + b * 16 : a * 128 + b * 16 + 16]
         remote(gst.at[1 - core, q], d0.at[q], d_send.at[q], d_recv.at[q], (sib, y)).start()
 
-    for q in (3, 2, 1):
+    def pair_sum(q):
         wait_bytes(d0.at[q], d_recv.at[q])
         hs[q - 1] = (gst[core, q] + d0[q]).astype(BF16)
         remote(hs.at[q - 1], hr.at[y], h_send.at[q - 1], h_recv.at[y], (me, order[q])).start()
+
+    multiply((2, 3))
+    gram(3)
+    gram(2)
+    pair_sum(3)
+    multiply((0, 1))
+    pair_sum(2)
+    gram(1)
+    gram(0)
+    pair_sum(1)
     wait_bytes(d0.at[0], d_recv.at[0])
     total = gst[core, 0] + d0[0]
     for yy in (y2, y3, y1):
@@ -359,9 +391,7 @@
         remote(tot.at[q], tr.at[p], t_send, t_recv, (q * 2 + core, y)).start()
     tr[p] = tot[p]
     wait_bytes(tr.at[pl.ds(0, 15)], t_recv)
-    final = jnp.sum(tr[...], axis=0)
-    stiff[...] = final[:, 0:128]
-    mass[...] = final[:, 128:256]
+    out[...] = jnp.sum(tr[...], axis=0)
 
     wait_bytes(send_m.at[pl.ds(0, 62)], sm_send)
     wait_bytes(rbuf.at[mine], w_send)
@@ -385,24 +415,13 @@
 
 
 def body(elem_records, elem_owner, elem_block, elem_offset, modes, mode_readers, pattern):
-    lane = lax.broadcasted_iota(I32, (256, 128), 1)
-    place = jnp.where(
-        lane == 0, elem_block[:, None], jnp.where(lane == 1, elem_offset[:, None], 0)
-    ).astype(BF16)
-    flat = mode_readers.reshape(-1)
-    ids = jnp.arange(32, dtype=I32)
-    rank = jnp.sum(((flat[:, None] == flat[None, :]) & (ids[:, None] < ids[None, :])).astype(I32), axis=0)
-    slot = flat * 2 + rank
-    hit = slot[None, :] == jnp.arange(NQ, dtype=I32)[:, None]
-    midx = jnp.sum(jnp.where(hit, ids[None, :] // 2 + 1, 0), axis=1) - 1
     dma = pltpu.SemaphoreType.DMA
     vm = pl.BlockSpec(memory_space=pltpu.VMEM)
-    sm = pl.BlockSpec(memory_space=pltpu.SMEM)
-    return pl.pallas_call(
+    out = pl.pallas_call(
         kernel,
-        out_shape=(jax.ShapeDtypeStruct((16, 128), F32), jax.ShapeDtypeStruct((16, 128), F32)),
-        in_specs=[sm, vm, vm, vm, vm, vm, vm],
-        out_specs=(vm, vm),
+        out_shape=jax.ShapeDtypeStruct((16, 256), F32),
+        in_specs=[vm] * 7,
+        out_specs=vm,
         scratch_shapes=[
             pltpu.VMEM((NQ, BS, COLS), BF16),
             pltpu.VMEM((5, NQ, BS, COLS), BF16),
@@ -422,13 +441,18 @@
             pltpu.VMEM((16, 16, 256), F32),
             dma, dma((16,)), dma, dma, dma, dma, dma, dma((16,)), dma, dma((4,)),
             dma, dma((16,)), dma((4,)), dma((4,)), dma((3,)), dma((4,)), dma, dma,
-            pltpu.VMEM((2, 128), I32), pltpu.SMEM((2, 128), I32), dma, dma, dma,
+            pltpu.VMEM((8, 128), I32), pltpu.VMEM((8, 128), I32), pltpu.SMEM((8, 128), I32), pltpu.SMEM((8, 128), I32),
+            dma, dma, dma, dma,
         ],
         compiler_params=pltpu.CompilerParams(
             collective_id=0, has_side_effects=True, vmem_limit_bytes=60 << 20
         ),
         name="sweep",
-    )(midx, pattern.reshape(2, 128), elem_records, place, elem_owner.reshape(1, 256), elem_owner, modes)
+    )(
+        pattern.T, elem_records, elem_owner.T, elem_block.reshape(1, 256), elem_offset.reshape(1, 256),
+        modes, mode_readers.T,
+    )
+    return out[:, 0:128], out[:, 128:256]
 
 
 def solution(mesh):

time: 95.1 us -> 85.3 us (0.90)
  Pallas kernels: 88.4 us -> 83.1 us
  local copies, waits for them, and re-layouts: 4.39 us -> 1.32 us
  other arithmetic: 1.47 us -> 0 us
    pallas_call x1, Pallas kernels: 88.4 us -> 83.1 us  [body(): pl.pallas_call(kernel, out_shape=jax.ShapeDtypeStruct((16, 256), F32), in...]
    unnamed x17 -> x0, local copies, waits for them, and re-layouts: 3.63 us -> none
    slice x0 -> x1, local copies, waits for them, and re-layouts: none -> 1.32 us  [body(): return (out[:, 0:128], out[:, 128:256])]
where the time goes in v3:
time: 85.3 us; the launch traced here: 85.1 us
  Pallas kernels  83.1 us (97%)
  local copies, waits for them, and re-layouts  1.32 us (2%)
    pallas_call x1, Pallas kernels, body(): pl.pallas_call(kernel, out_shape=jax.ShapeDtypeStruct((16, 256), F32), in...  83.1 us

profile of v3, /device:TPU:1, one launch (start us, length us, event | category | flops | bytes accessed | tf_op | source)
XLA Modules:
  0.0 85.1 jit_solution(15706037671860743142)
XLA Ops:
  0.6 83.1 %sweep.1 = f32[16,256]{1,0:T(8,128)} custom-call(s32[4,64]{1,0:T(4,128)} %bitcast.5, bf16[256,1152]{1,0:T(8,128)(2,1)} %rec.1, s32[1,256]{1,0:T(1,128)} %bitcast.6, s32[1,256]{1,0:T(1,128)} %bitcast.7, s32[1,256]{1,0:T(1,128)} %bitcast.8, bf16[16,64,128]{2,1,0:T(8,128)(2,1)} %modes.1, s32[2,16]{1,0:T(2,128)} %bitcast.9), custom_call_target="tpu_custom_call" | custom-call | tf_op jit(solution)/shard_map/sweep/pallas_call | solution.py:420
  83.8 1.3 %fusion = (f32[16,128]{1,0:T(8,128)}, f32[16,128]{1,0:T(8,128)}) fusion(f32[16,256]{1,0:T(8,128)} %sweep.1), kind=kLoop, calls=%fused_computation | loop fusion | bytes 32768 | tf_op jit(solution)/shard_map/slice | solution.py:455

commit v4 on v3

--- a/solution.py
+++ b/solution.py
@@ -226,8 +226,8 @@
     chips = [p] + [chip_at((4 - dz) % 4, (4 - dx) % 4) for dz, dx in FAR]
     for n, q in enumerate(chips):
         first(q, xf.at[own, pl.ds(2 * sib, 2)] if n == 0 else xf.at[own, pl.ds(4 * q, 4)])
-    for dz, dx in FAR:
-        for cc in range(2):
+    for cc in (host, 1 - host):
+        for dz, dx in FAR:
             send_rec(chip_at(dz, dx), cc)
 
     def place_matrix(n, _):
@@ -241,8 +241,6 @@
         return 0
 
     lax.fori_loop(0, 24, place_matrix, 0)
-    for o in (0, 1, 8, 9):
-        mbuf[o] = jnp.zeros((128, KA), BF16)
 
     for q in chips:
         second(q)
@@ -299,25 +297,27 @@
     row = (blk >> 2) - 32 * core
     key = jnp.where((row >= 0) & (row < 32), where[1:2] * 128 + (blk & 3) * 32 + row, -1)
 
-    def collect(o, _):
+    def collect(o):
         rows = lax.broadcasted_iota(I32, (128, 1024), 0) + o * 128
         pick = jnp.where(rows == key, 1.0, 0.0).astype(BF16)
-        mbuf[o + 2] = dot(pick, rbuf[...]).astype(BF16)
-        return 0
-
-    lax.fori_loop(0, 6, collect, 0)
-
-    def assemble(v, _):
+        mbuf[o] = dot(pick, rbuf[...]).astype(BF16)
+
+    for o in range(6):
+        collect(o)
+
+    def assemble(v):
         for c in range(2):
             for w in range(2):
                 acc = None
                 for d in range(3):
+                    if not 0 <= v - d <= 5:
+                        continue
                     start = c * 576 + 96 * (w + 2 * d)
                     base = start // 128 * 128
                     ri = (start - base) // 32
                     term = dot(
-                        mbuf[v - d + 2, :, base : base + 256],
-                        ebuf[ri * 6 + jnp.clip(v - d, 0, 5)],
+                        mbuf[v - d, :, base : base + 256],
+                        ebuf[ri * 6 + v - d],
                     )
                     acc = term if acc is None else acc + term
                 acc = acc.astype(BF16)
@@ -325,9 +325,9 @@
                     ks[c * 64 + 8 * v + 4 * w + a4] = jnp.concatenate(
                         [acc[j * 32 : j * 32 + 32, a4 * 64 : a4 * 64 + 64] for j in range(4)], axis=1
                     )
-        return 0
-
-    lax.fori_loop(0, 8, assemble, 0)
+
+    for v in range(8):
+        assemble(v)
 
     r0 = lax.broadcasted_iota(I32, (256, 256), 0)
     r1 = lax.broadcasted_iota(I32, (256, 256), 1)
@@ -428,7 +428,7 @@
             pltpu.VMEM((512, KA), BF16),
             pltpu.VMEM((1024, KA), BF16),
             pltpu.VMEM((24, 256, 256), BF16),
-            pltpu.VMEM((10, 128, KA), BF16),
+            pltpu.VMEM((6, 128, KA), BF16),
             pltpu.VMEM((128, 32, 256), BF16),
             pltpu.VMEM((32, 128, 256), BF16),
             pltpu.VMEM((512, 2048), BF16),

time: 85.3 us -> 77.4 us (0.907)
  Pallas kernels: 83.1 us -> 75.2 us
    pallas_call x1, Pallas kernels: 83.1 us -> 75.2 us  [body(): pl.pallas_call(kernel, out_shape=jax.ShapeDtypeStruct((16, 256), F32), in...]
where the time goes in v4:
time: 77.4 us; the launch traced here: 77.2 us
  Pallas kernels  75.2 us (97%)
  local copies, waits for them, and re-layouts  1.32 us (2%)
    pallas_call x1, Pallas kernels, body(): pl.pallas_call(kernel, out_shape=jax.ShapeDtypeStruct((16, 256), F32), in...  75.2 us

profile of v4, /device:TPU:1, one launch (start us, length us, event | category | flops | bytes accessed | tf_op | source)
XLA Modules:
  0.0 77.2 jit_solution(10261884937604860400)
XLA Ops:
  0.6 75.2 %sweep.1 = f32[16,256]{1,0:T(8,128)} custom-call(s32[4,64]{1,0:T(4,128)} %bitcast.5, bf16[256,1152]{1,0:T(8,128)(2,1)} %rec.1, s32[1,256]{1,0:T(1,128)} %bitcast.6, s32[1,256]{1,0:T(1,128)} %bitcast.7, s32[1,256]{1,0:T(1,128)} %bitcast.8, bf16[16,64,128]{2,1,0:T(8,128)(2,1)} %modes.1, s32[2,16]{1,0:T(2,128)} %bitcast.9), custom_call_target="tpu_custom_call" | custom-call | tf_op jit(solution)/shard_map/sweep/pallas_call | solution.py:420
  75.9 1.3 %fusion = (f32[16,128]{1,0:T(8,128)}, f32[16,128]{1,0:T(8,128)}) fusion(f32[16,256]{1,0:T(8,128)} %sweep.1), kind=kLoop, calls=%fused_computation | loop fusion | bytes 32768 | tf_op jit(solution)/shard_map/slice | solution.py:455

commit v5 on v4

--- a/solution.py
+++ b/solution.py
@@ -40,7 +40,7 @@
     out,
     send_m, xf, send_r, rbuf, ebuf, mbuf, ks, lb, xt, pb, gst, d0, hs, hr, tot, tr,
     sm_send, a_recv, r_send, r_recv, w_send, w_recv, b_send, b_recv, c_send, c_recv,
-    e_send, e_recv, d_send, d_recv, h_send, h_recv, t_send, t_recv, tab, patv, pats, mids, p_send, p_recv, p_copy, m_copy,
+    e_send, e_recv, d_send, d_recv, h_send, h_recv, t_send, t_recv, tab, patv, pats, mids, p_send, p_recv, p_copy, m_copy, half,
 ):
     me = lax.axis_index("sub")
     y = lax.axis_index("col")
@@ -254,6 +254,17 @@
         here.start()
         here.wait()
 
+    @pl.when(guest == 0)
+    def _():
+        wait_bytes(rbuf.at[pl.ds(0, 31 * 16)], r_recv)
+
+    @pl.when(guest == 1)
+    def _():
+        wait_bytes(rbuf.at[pl.ds(0, 32 * 16)], r_recv)
+
+    mine = pl.ds(pl.multiple_of(512 * guest, 512), 512)
+    remote(rbuf.at[mine], rbuf.at[mine], w_send, w_recv, (sib, y)).start()
+
     turned = eye(128)
 
     def transpose(k):
@@ -262,7 +273,7 @@
             xt[k * 128 : k * 128 + 128, pl.ds(pl.multiple_of(g * 256, 256), 256)] = dot_nt(turned, part).astype(BF16)
             return 0
 
-        lax.fori_loop(0, 8, one, 0, unroll=4)
+        lax.fori_loop(0, 8, one, 0, unroll=8)
 
     @pl.when(guest == 0)
     def _():
@@ -277,33 +288,24 @@
     for k in range(4):
         transpose(k)
 
-    @pl.when(guest == 0)
-    def _():
-        wait_bytes(rbuf.at[pl.ds(0, 31 * 16)], r_recv)
-
-    @pl.when(guest == 1)
-    def _():
-        wait_bytes(rbuf.at[pl.ds(0, 32 * 16)], r_recv)
-
-    mine = pl.ds(pl.multiple_of(512 * guest, 512), 512)
-    remote(rbuf.at[mine], rbuf.at[mine], w_send, w_recv, (sib, y)).start()
+    pickrow = jnp.where(iota((8, 128), 0) == iota((8, 128), 1), 1.0, 0.0).astype(BF16)
+
+    def collect(rows, last):
+        facts = dot_nt(pickrow, rbuf[rows, KW:KA]).astype(I32)
+        blk = facts[0:1]
+        row = (blk >> 2) - 32 * core
+        key = jnp.where((row >= 0) & (row < 32), facts[1:2] * 128 + (blk & 3) * 32 + row, -1)
+        for o in range(6):
+            pick = jnp.where(iota((128, 512), 0) + o * 128 == key, 1.0, 0.0).astype(BF16)
+            part = dot(pick, rbuf[rows, :])
+            if last:
+                mbuf[o] = (half[o] + part).astype(BF16)
+            else:
+                half[o] = part
+
+    collect(mine, False)
     wait_bytes(rbuf.at[pl.ds(pl.multiple_of(512 * (1 - guest), 512), 512)], w_recv)
-
-    lane = lax.broadcasted_iota(I32, (8, 128), 1)
-    rowi = lax.broadcasted_iota(I32, (8, 128), 0)
-    pickrow = jnp.where(lane == rowi, 1.0, 0.0).astype(BF16)
-    where = dot_nt(pickrow, rbuf[:, KW:KA]).astype(I32)
-    blk = where[0:1]
-    row = (blk >> 2) - 32 * core
-    key = jnp.where((row >= 0) & (row < 32), where[1:2] * 128 + (blk & 3) * 32 + row, -1)
-
-    def collect(o):
-        rows = lax.broadcasted_iota(I32, (128, 1024), 0) + o * 128
-        pick = jnp.where(rows == key, 1.0, 0.0).astype(BF16)
-        mbuf[o] = dot(pick, rbuf[...]).astype(BF16)
-
-    for o in range(6):
-        collect(o)
+    collect(pl.ds(pl.multiple_of(512 * (1 - guest), 512), 512), True)
 
     def assemble(v):
         for c in range(2):
@@ -340,7 +342,7 @@
         lb[irow, arow, :] = dot(swap, part).astype(BF16).reshape(16, 16, 256)
         return 0
 
-    lax.fori_loop(0, 16, turn, 0, unroll=2)
+    lax.fori_loop(0, 16, turn, 0, unroll=8)
 
     def multiply(kinds):
         def one(i, _):
@@ -355,7 +357,7 @@
                 pb[k, at, 128:256] = out[64:128, n * 128 : n * 128 + 128]
             return 0
 
-        lax.fori_loop(0, 32, one, 0, unroll=4)
+        lax.fori_loop(0, 32, one, 0, unroll=8)
 
     def gram(q):
         g = dot(xt[...], pb[q])
@@ -377,8 +379,8 @@
     multiply((0, 1))
     pair_sum(2)
     gram(1)
+    pair_sum(1)
     gram(0)
-    pair_sum(1)
     wait_bytes(d0.at[0], d_recv.at[0])
     total = gst[core, 0] + d0[0]
     for yy in (y2, y3, y1):
@@ -442,7 +444,7 @@
             dma, dma((16,)), dma, dma, dma, dma, dma, dma((16,)), dma, dma((4,)),
             dma, dma((16,)), dma((4,)), dma((4,)), dma((3,)), dma((4,)), dma, dma,
             pltpu.VMEM((8, 128), I32), pltpu.VMEM((8, 128), I32), pltpu.SMEM((8, 128), I32), pltpu.SMEM((8, 128), I32),
-            dma, dma, dma, dma,
+            dma, dma, dma, dma, pltpu.VMEM((6, 128, KA), F32),
         ],
         compiler_params=pltpu.CompilerParams(
             collective_id=0, has_side_effects=True, vmem_limit_bytes=60 << 20

time: 77.4 us -> 73.7 us (0.952)
  Pallas kernels: 75.2 us -> 71.5 us
    pallas_call x1, Pallas kernels: 75.2 us -> 71.5 us  [body(): pl.pallas_call(kernel, out_shape=jax.ShapeDtypeStruct((16, 256), F32), in...]
where the time goes in v5:
time: 73.7 us; the launch traced here: 73.5 us
  Pallas kernels  71.5 us (97%)
  local copies, waits for them, and re-layouts  1.32 us (2%)
    pallas_call x1, Pallas kernels, body(): pl.pallas_call(kernel, out_shape=jax.ShapeDtypeStruct((16, 256), F32), in...  71.5 us

profile of v5, /device:TPU:1, one launch (start us, length us, event | category | flops | bytes accessed | tf_op | source)
XLA Modules:
  0.0 73.5 jit_solution(4858486924710932091)
XLA Ops:
  0.6 71.5 %sweep.1 = f32[16,256]{1,0:T(8,128)} custom-call(s32[4,64]{1,0:T(4,128)} %bitcast.5, bf16[256,1152]{1,0:T(8,128)(2,1)} %rec.1, s32[1,256]{1,0:T(1,128)} %bitcast.6, s32[1,256]{1,0:T(1,128)} %bitcast.7, s32[1,256]{1,0:T(1,128)} %bitcast.8, bf16[16,64,128]{2,1,0:T(8,128)(2,1)} %modes.1, s32[2,16]{1,0:T(2,128)} %bitcast.9), custom_call_target="tpu_custom_call" | custom-call | tf_op jit(solution)/shard_map/sweep/pallas_call | solution.py:422
  72.2 1.3 %fusion = (f32[16,128]{1,0:T(8,128)}, f32[16,128]{1,0:T(8,128)}) fusion(f32[16,256]{1,0:T(8,128)} %sweep.1), kind=kLoop, calls=%fused_computation | loop fusion | bytes 32768 | tf_op jit(solution)/shard_map/slice | solution.py:457

commit v6 on v5

--- a/solution.py
+++ b/solution.py
@@ -270,10 +270,13 @@
     def transpose(k):
         def one(g, _):
             part = xf[k, pl.ds(32 * core + 4 * g, 4)].reshape(256, COLS)
-            xt[k * 128 : k * 128 + 128, pl.ds(pl.multiple_of(g * 256, 256), 256)] = dot_nt(turned, part).astype(BF16)
+            xt[pl.ds(pl.multiple_of(k * 128, 128), 128), pl.ds(pl.multiple_of(g * 256, 256), 256)] = dot_nt(turned, part).astype(BF16)
             return 0
 
         lax.fori_loop(0, 8, one, 0, unroll=8)
+
+    transpose(2 * guest)
+    transpose(2 * guest + 1)
 
     @pl.when(guest == 0)
     def _():
@@ -285,8 +288,8 @@
         wait_bytes(xf.at[0], c_recv.at[0])
         wait_bytes(xf.at[1], c_recv.at[1])
 
-    for k in range(4):
-        transpose(k)
+    transpose(2 - 2 * guest)
+    transpose(3 - 2 * guest)
 
     pickrow = jnp.where(iota((8, 128), 0) == iota((8, 128), 1), 1.0, 0.0).astype(BF16)
 
@@ -357,7 +360,7 @@
                 pb[k, at, 128:256] = out[64:128, n * 128 : n * 128 + 128]
             return 0
 
-        lax.fori_loop(0, 32, one, 0, unroll=8)
+        lax.fori_loop(0, 32, one, 0, unroll=16)
 
     def gram(q):
         g = dot(xt[...], pb[q])

time: 73.7 us -> 73.4 us (level)
  no operation moved by 1% of the time
where the time goes in v6:
time: 73.4 us; the launch traced here: 73.2 us
  Pallas kernels  71.2 us (97%)
  local copies, waits for them, and re-layouts  1.32 us (2%)
    pallas_call x1, Pallas kernels, body(): pl.pallas_call(kernel, out_shape=jax.ShapeDtypeStruct((16, 256), F32), in...  71.2 us

profile of v6, /device:TPU:1, one launch (start us, length us, event | category | flops | bytes accessed | tf_op | source)
XLA Modules:
  0.0 73.2 jit_solution(6158823813565875619)
XLA Ops:
  0.6 71.2 %sweep.1 = f32[16,256]{1,0:T(8,128)} custom-call(s32[4,64]{1,0:T(4,128)} %bitcast.5, bf16[256,1152]{1,0:T(8,128)(2,1)} %rec.1, s32[1,256]{1,0:T(1,128)} %bitcast.6, s32[1,256]{1,0:T(1,128)} %bitcast.7, s32[1,256]{1,0:T(1,128)} %bitcast.8, bf16[16,64,128]{2,1,0:T(8,128)(2,1)} %modes.1, s32[2,16]{1,0:T(2,128)} %bitcast.9), custom_call_target="tpu_custom_call" | custom-call | tf_op jit(solution)/shard_map/sweep/pallas_call | solution.py:425
  71.9 1.3 %fusion = (f32[16,128]{1,0:T(8,128)}, f32[16,128]{1,0:T(8,128)}) fusion(f32[16,256]{1,0:T(8,128)} %sweep.1), kind=kLoop, calls=%fused_computation | loop fusion | bytes 32768 | tf_op jit(solution)/shard_map/slice | solution.py:460

commit v7 on v5

--- a/solution.py
+++ b/solution.py
@@ -114,6 +114,53 @@
     to_mids = pltpu.make_async_copy(tab, mids, m_copy)
     to_mids.start()
 
+    to_mids.wait()
+
+    def fill(s, _):
+        k = mids[4 + lax.rem(s, 2), s // 2]
+        block = modes[jnp.clip(k, 0, modes.shape[0] - 1)]
+        send_m[s] = jnp.where(k >= 0, block, jnp.zeros_like(block))
+        return 0
+
+    lax.fori_loop(0, NQ, fill, 0, unroll=4)
+
+    pl.semaphore_wait(barrier, 53)
+
+    xf[own, pl.ds(2 * me, 2)] = send_m[pl.ds(2 * me, 2)]
+
+    @pl.when(guest == 0)
+    def _():
+        away = remote(tab, patv, p_send, p_recv, (sib, y))
+        away.start()
+        here = pltpu.make_async_copy(tab, pats, p_copy)
+        here.start()
+        away.wait_send()
+        here.wait()
+
+    def other(cc):
+        return lax.rem(cc + host, 2)
+
+    def send_mode(dest, lands):
+        remote(
+            send_m.at[pl.ds(2 * dest, 2)], xf.at[lands, pl.ds(2 * me, 2)], sm_send, a_recv.at[p], (dest, y)
+        ).start()
+
+    def rows16(n):
+        return pl.ds(pl.multiple_of(n * 16, 16), 16)
+
+    def send_rec(q, cc):
+        far = other(cc)
+        remote(
+            send_r.at[rows16(q * 2 + cc)], rbuf.at[rows16(32 * far + me)], r_send, r_recv,
+            (q * 2 + host, y + far * (y3 - y)),
+        ).start()
+
+    send_mode(sib, 4 * (1 - guest))
+    for dz, dx in FAR:
+        q = chip_at(dz, dx)
+        for cc in range(2):
+            send_mode(q * 2 + cc, 4 * other(cc))
+
     lines = iota((128, 256), 0)
     facts = jnp.where(
         lines == 0, block_row[...], jnp.where(lines == 1, offset_row[...], jnp.where(lines == 2, owner_row[...], 0))
@@ -133,53 +180,6 @@
         return 0
 
     lax.fori_loop(0, 4, permute, 0)
-
-    to_mids.wait()
-
-    def fill(s, _):
-        k = mids[4 + lax.rem(s, 2), s // 2]
-        block = modes[jnp.clip(k, 0, modes.shape[0] - 1)]
-        send_m[s] = jnp.where(k >= 0, block, jnp.zeros_like(block))
-        return 0
-
-    lax.fori_loop(0, NQ, fill, 0, unroll=4)
-
-    pl.semaphore_wait(barrier, 53)
-
-    xf[own, pl.ds(2 * me, 2)] = send_m[pl.ds(2 * me, 2)]
-
-    @pl.when(guest == 0)
-    def _():
-        away = remote(tab, patv, p_send, p_recv, (sib, y))
-        away.start()
-        here = pltpu.make_async_copy(tab, pats, p_copy)
-        here.start()
-        away.wait_send()
-        here.wait()
-
-    def other(cc):
-        return lax.rem(cc + host, 2)
-
-    def send_mode(dest, lands):
-        remote(
-            send_m.at[pl.ds(2 * dest, 2)], xf.at[lands, pl.ds(2 * me, 2)], sm_send, a_recv.at[p], (dest, y)
-        ).start()
-
-    def rows16(n):
-        return pl.ds(pl.multiple_of(n * 16, 16), 16)
-
-    def send_rec(q, cc):
-        far = other(cc)
-        remote(
-            send_r.at[rows16(q * 2 + cc)], rbuf.at[rows16(32 * far + me)], r_send, r_recv,
-            (q * 2 + host, y + far * (y3 - y)),
-        ).start()
-
-    send_mode(sib, 4 * (1 - guest))
-    for dz, dx in FAR:
-        q = chip_at(dz, dx)
-        for cc in range(2):
-            send_mode(q * 2 + cc, 4 * other(cc))
 
     @pl.when(guest == 0)
     def _():

time: 73.7 us -> 73.6 us (level)
  no operation moved by 1% of the time
where the time goes in v7:
time: 73.6 us; the launch traced here: 73.4 us
  Pallas kernels  71.5 us (97%)
  local copies, waits for them, and re-layouts  1.32 us (2%)
    pallas_call x1, Pallas kernels, body(): pl.pallas_call(kernel, out_shape=jax.ShapeDtypeStruct((16, 256), F32), in...  71.5 us

profile of v7, /device:TPU:1, one launch (start us, length us, event | category | flops | bytes accessed | tf_op | source)
XLA Modules:
  0.0 73.4 jit_solution(1006707577645176200)
XLA Ops:
  0.6 71.5 %sweep.1 = f32[16,256]{1,0:T(8,128)} custom-call(s32[4,64]{1,0:T(4,128)} %bitcast.5, bf16[256,1152]{1,0:T(8,128)(2,1)} %rec.1, s32[1,256]{1,0:T(1,128)} %bitcast.6, s32[1,256]{1,0:T(1,128)} %bitcast.7, s32[1,256]{1,0:T(1,128)} %bitcast.8, bf16[16,64,128]{2,1,0:T(8,128)(2,1)} %modes.1, s32[2,16]{1,0:T(2,128)} %bitcast.9), custom_call_target="tpu_custom_call" | custom-call | tf_op jit(solution)/shard_map/sweep/pallas_call | solution.py:422
  72.1 1.3 %fusion = (f32[16,128]{1,0:T(8,128)}, f32[16,128]{1,0:T(8,128)}) fusion(f32[16,256]{1,0:T(8,128)} %sweep.1), kind=kLoop, calls=%fused_computation | loop fusion | bytes 32768 | tf_op jit(solution)/shard_map/slice | solution.py:457
